TPU v7x, 1024 devices: a whole 4x8x16 slice. The times are simulated.
1024 devices in a mesh: section: 16 (over z_hi, x), st: 16 (over y, core), dp: 4 (over z_lo).
Axes of the slice: x: 4, y: 8, z: 16 (z_hi: 4, z_lo: 4; z = z_hi * 4 + z_lo), core: 2. Of those that a mesh axis runs over, the one named last changes fastest.
Arguments:
- saved_qkv: bfloat16 [16, 4, 3, 128, 48, 128], P('section', 'dp', None, None, 'st'), may hold values from -9 to 9
- positions: int32 [16, 4, 128], P('section', 'dp'), may hold values from 0 to 127, as said below
- w_out: bfloat16 [16, 6144, 6144], P('section', None, 'st'), may hold values from -0.078125 to 0.078125
- grad_out: bfloat16 [16, 4, 128, 6144], P('section', 'dp', None, 'st'), may hold values from -6 to 6
Outputs:
- grad_weight: bfloat16 [16, 6144, 6144], P('section', 'dp', 'st')
- upstream: bfloat16 [16, 4, 3, 128, 48, 128], P('section', 'dp', None, None, 'st')
Inputs may be any that keep to these rules, and one draw needn't show every extreme that they name: `positions`: each row holds every number 0 to 127 once.
All inputs are finite; a program needn't handle non-finite values.
Results may differ from a plain program's by a relative error of at most 0.0095.
Values may be sent and summed in bfloat16 or wider, within the bound.
A program may use at most 32 MiB of HBM per device.

v0:
```python
import math

import jax
import jax.numpy as jnp
from jax import lax
from jax.sharding import PartitionSpec as P


def from_behind(value, axis, steps):
    count = lax.axis_size(axis)
    initial, last = (max(0, -steps), min(count, count - steps))
    return lax.ppermute(value, axis, [(source, source + steps) for source in range(initial, last)])


def local(saved_qkv, positions, w_out, grad_out):
    head_major = saved_qkv[0, 0]
    queries = head_major[0]
    key_rows = head_major[1]
    values = head_major[2]
    token_pos = positions[0, 0]
    inv_root = 1.0 / math.sqrt(queries.shape[-1])
    scores = (
        jnp.einsum("qhd,khd->hqk", queries, key_rows, preferred_element_type=jnp.float32) * inv_root
    )
    visible = token_pos[None, :] <= token_pos[:, None]
    scores = jnp.where(visible[None], scores, -1e30)
    highest = jnp.max(scores, axis=2, keepdims=True)
    exponent = jnp.exp(scores - highest)
    softmax_out = exponent / jnp.sum(exponent, axis=2, keepdims=True)
    weights_bf = softmax_out.astype(jnp.bfloat16)
    attended = jnp.einsum(
        "hqk,khd->qhd", weights_bf, values, preferred_element_type=jnp.float32
    ).astype(jnp.bfloat16)
    seq_len = attended.shape[0]
    flat_att = attended.reshape(seq_len, -1)
    full_grad = lax.all_gather(grad_out[0, 0], "st", axis=1, tiled=True)
    d_flat = jnp.dot(full_grad, w_out[0], preferred_element_type=jnp.float32).astype(jnp.bfloat16)
    summed = lax.psum_scatter(
        lax.dot_general(
            full_grad, flat_att, (((0,), (0,)), ((), ())), preferred_element_type=jnp.float32
        ).astype(jnp.bfloat16),
        "dp",
        scatter_dimension=0,
        tiled=True,
    )
    d_heads = d_flat.reshape(attended.shape)
    d_values = jnp.einsum(
        "hqk,qhd->khd", weights_bf, d_heads, preferred_element_type=jnp.float32
    ).astype(jnp.bfloat16)
    d_weights = jnp.einsum("qhd,khd->hqk", d_heads, values, preferred_element_type=jnp.float32)
    row_dot = jnp.sum(softmax_out * d_weights, axis=2, keepdims=True)
    d_scores = (softmax_out * (d_weights - row_dot)).astype(jnp.bfloat16)
    d_queries = (
        jnp.einsum("hqk,khd->qhd", d_scores, key_rows, preferred_element_type=jnp.float32)
        * inv_root
    ).astype(jnp.bfloat16)
    d_keys = (
        jnp.einsum("hqk,qhd->khd", d_scores, queries, preferred_element_type=jnp.float32) * inv_root
    ).astype(jnp.bfloat16)
    stacked = jnp.stack([d_queries, d_keys, d_values])[None, None]
    received = from_behind(stacked, "section", -1)
    return (summed[None], received)


def solution(mesh):
    in_specs = (
        P("section", "dp", None, None, "st", None),
        P("section", "dp", None),
        P("section", None, "st"),
        P("section", "dp", None, "st"),
    )
    out_specs = (P("section", "dp", "st"), P("section", "dp", None, None, "st", None))
    return jax.shard_map(local, mesh=mesh, in_specs=in_specs, out_specs=out_specs, check_vma=False)
```

profile of v0, /device:TPU:1, one launch (start us, length us, event | category | flops | bytes accessed | tf_op | source)
XLA Modules:
  0.0 192.9 jit_solution(12640712668803936595)
XLA Ops:
  7.2 0.0 all-gather.3.cloned.1.call-start
  7.2 0.7 all-gather.3.cloned.1.call-update
  7.9 0.0 reduce-scatter.2.cloned.1.call-start
  7.9 0.8 broadcast_compare_fusion
  8.8 1.1 fusion.7
  9.9 0.2 fusion.34
  10.1 1.1 convolution_convert_fusion.1
  11.2 55.1 %all-gather.3.cloned.1.call-done = bf16[1,1,128,6144]{3,2,1,0:T(8,128)(2,1)} async-done(((bf16[1,1,128,384]{3,2,1,0:T(8,128)(2,1)}), bf16[1,1,128,6144]{3,2,1,0:T(8,128)(2,1)}) %all-gather.3.cloned.1.call-update) | async-done | bytes 1572880 | tf_op jit(solution)/shard_map/all_gather | solution.py:36
  66.4 4.9 %fusion.1 = bf16[6144,384]{0,1:T(8,128)(2,1)} fusion(bf16[128,384]{0,1:T(8,128)(2,1)S(1)} %bitcast.62, bf16[1,1,128,6144]{3,2,1,0:T(8,128)(2,1)} %all-gather.3.cloned.1.call-done), kind=kOutput, calls=%fused_computation.2 | convolution fusion | flops 606339072 | bytes 6389760 | tf_op jit(solution)/shard_map/dot_general | solution.py:39
  71.3 0.0 copy-start
  71.3 0.0 reduce-scatter.2.cloned.1.call-update
  71.3 1.4 copy-done
  72.7 0.0 copy-start.1
  72.7 3.4 %fusion.11 = bf16[128,384]{1,0:T(8,128)(2,1)S(1)} fusion(bf16[1,6144,384]{2,1,0:T(8,128)(2,1)} %param.6, bf16[1,1,128,6144]{3,2,1,0:T(8,128)(2,1)S(1)} %copy-done), kind=kOutput, calls=%fused_computation.15 | convolution fusion | flops 604028928 | bytes 6389760 | tf_op jit(solution)/shard_map/dot_general | solution.py:37
  76.0 0.1 copy.19
  76.2 0.2 fusion.16
  76.4 0.0 copy-done.1
  76.4 0.2 multiply_reduce_fusion
  76.7 0.2 fusion.17
  76.9 0.2 fusion.18
  77.2 1.3 collective-permute-start
  78.5 9.0 %collective-permute-done = bf16[1,1,3,128,3,128]{3,5,4,2,1,0:T(8,128)(2,1)S(1)} collective-permute-done((bf16[1,1,3,128,3,128]{3,5,4,2,1,0:T(8,128)(2,1)S(1)}, bf16[1,1,3,128,3,128]{3,5,4,2,1,0:T(8,128)(2,1)S(1)}, u32[]{:S(2)}, u32[]{:S(2)}) %collective-permute-start) | collective-permute-done | bytes 294944 | tf_op jit(solution)/shard_map/ppermute | solution.py:12
  87.5 0.9 copy.27
  88.3 95.4 %reduce-scatter.2.cloned.1.call-done = bf16[1536,384]{0,1:T(8,128)(2,1)} async-done(((bf16[6144,384]{0,1:T(8,128)(2,1)}), bf16[1536,384]{0,1:T(8,128)(2,1)}) %reduce-scatter.2.cloned.1.call-update) | async-done | bytes 1179664 | tf_op jit(solution)/shard_map/reduce_scatter | solution.py:38
  183.7 2.4 %copy.26 = bf16[1,1536,384]{2,1,0:T(8,128)(2,1)} copy(bf16[1,1536,384]{1,2,0:T(8,128)(2,1)} %bitcast.61) | data formatting | bytes 2359296
  (2 shorter events, 0.1 us)
Async XLA Ops:
  7.2 59.2 %all-gather.3.cloned.1.call-start = ((), (), s32[]{:S(2)}) async-start(), calls=%async_computation.2 | async-start | bytes 1671168 | tf_op jit(solution)/shard_map/all_gather | solution.py:36
  7.9 175.8 %reduce-scatter.2.cloned.1.call-start = ((), (), s32[]{:S(2)}) async-start(), calls=%async_computation.1 | async-start | bytes 5898240 | tf_op jit(solution)/shard_map/reduce_scatter | solution.py:38
  71.3 1.4 copy-start
  72.7 3.7 %copy-start.1 = (bf16[1,1,3,128,3,128]{5,3,4,2,1,0:T(8,128)(2,1)S(1)}, bf16[1,1,3,128,3,128]{5,3,4,2,1,0:T(8,128)(2,1)}, u32[]{:S(2)}) copy-start(bf16[1,1,3,128,3,128]{5,3,4,2,1,0:T(8,128)(2,1)} %param.4) | copy-start | bytes 884740
  77.2 10.3 %collective-permute-start = (bf16[1,1,3,128,3,128]{3,5,4,2,1,0:T(8,128)(2,1)S(1)}, bf16[1,1,3,128,3,128]{3,5,4,2,1,0:T(8,128)(2,1)S(1)}, u32[]{:S(2)}, u32[]{:S(2)}) collective-permute-start(bf16[1,1,3,128,3,128]{3,5,4,2,1,0:T(8,128)(2,1)S(1)} %maximum_bitcast_fusion), channel_id=1, source_target_pairs={{64,0},{128,64},{192,128},{256,192},{320,256},{384,320},{448,384},... | collective-permute-start | bytes 884744 | tf_op jit(solution)/shard_map/ppermute | solution.py:12
Sparse Core Ops, SparseCore 0:
  10.7 55.6 all-gather.2
  71.4 112.2 reduce-scatter.1
where the time goes:
time: 193 us
  waiting for transfers between devices  160 us (83%)
  between operations  14.1 us (7%)
  matrix products  11.4 us (6%)
  local copies, waits for them, and re-layouts  4.77 us (2%)
    reduce_scatter x1, waiting for transfers between devices, local(): lax.psum_scatter(lax.dot_general(full_grad, flat_att, (((0,), (0,)), ((),...  95.4 us
    all_gather x1, waiting for transfers between devices, local(): full_grad = lax.all_gather(grad_out[0, 0], 'st', axis=1, tiled=True)  55.1 us
    ppermute x1, waiting for transfers between devices, from_behind(): lax.ppermute(value, axis, [(source, source + steps) for source in range(i...  8.95 us
    dot_general x1, matrix products, local(): lax.dot_general(full_grad, flat_att, (((0,), (0,)), ((), ())), preferred_...  4.91 us
    unnamed x6, local copies, waits for them, and re-layouts  4.65 us
  transfers between devices with their start and end apart: 3, of which 3 were waited for; matrix products, arithmetic and copies ran while one was open for 4% of the time, Pallas kernels for 0%

commit v1 on v0

v1 whole, which is shorter than its diff:
```python
import math

import jax
import jax.numpy as jnp
from jax import lax
from jax.experimental import pallas as pl
from jax.experimental.pallas import tpu as pltpu
from jax.sharding import PartitionSpec as P

MESH = pl.DeviceIdType.MESH
F32, BF16 = jnp.float32, jnp.bfloat16
SEQ, DH, NH, COLS = 128, 128, 3, 384
HALF = SEQ // 2
VMEM_LIMIT = 56 * 2**20


def dot(a, b, ca, cb):
    return lax.dot_general(a, b, (((ca,), (cb,)), ((), ())), preferred_element_type=F32)


def probs_t(qkv, pos, h):
    scores = dot(qkv[NH + h], qkv[h], 1, 1) * (1.0 / math.sqrt(DH))
    pos_q = jnp.broadcast_to(pos[...], (SEQ, SEQ))
    scores = jnp.where(pos_q.T <= pos_q, scores, -1e30)
    e = jnp.exp(scores - jnp.max(scores, axis=0, keepdims=True))
    return e / jnp.sum(e, axis=0, keepdims=True)


def kernel(
    qkv_in, pos_in, w_in, grad_in, dw_out, up_out,
    gath, w_v, qkv_o, pos_o, qkv_u, pos_u, relay, relay2, att, gd, acc, d_own, d_up, p_up,
    loc, g_s, g_r, b_s, b_r, z_s, z_r, a_s, a_r, e_s, e_r, l_s, l_r, x_s, x_r,
):
    s, t, d = lax.axis_index("section"), lax.axis_index("st"), lax.axis_index("dp")
    y, c = t // 2, t % 2
    x, hi = s % 4, s // 4
    base = hi * 4
    sib = y * 2 + 1 - c
    crosses = hi > 0

    def row(j, core=None):
        return lax.rem(y + 8 + j, 8) * 2 + (c if core is None else core)

    def remote(src, dst, ss, rs, dev):
        return pltpu.make_async_remote_copy(
            src_ref=src, dst_ref=dst, send_sem=ss, recv_sem=rs, device_id=dev, device_id_type=MESH
        )

    bar = pltpu.get_barrier_semaphore()

    def greet(dev):
        pl.semaphore_signal(bar, inc=1, device_id=dev, device_id_type=MESH)

    for j in (1, -1, 2, -2):
        greet((s, row(j), d))
    greet((s, sib, d))
    for i in (1, 2, 3):
        greet((s, t, lax.rem(d + i, 4)))
        greet((base + lax.rem(x + i, 4), t, d))

    @pl.when(jnp.logical_and(x == 3, hi < 3))
    def _():
        for i in range(4):
            greet((base + 4 + i, t, d))

    locals_ = [
        pltpu.make_async_copy(qkv_in, qkv_o, loc.at[0]),
        pltpu.make_async_copy(pos_in, pos_o, loc.at[1]),
        pltpu.make_async_copy(grad_in, gath.at[t], loc.at[2]),
        pltpu.make_async_copy(w_in, w_v, loc.at[3]),
    ]
    for copy in locals_:
        copy.start()

    pl.semaphore_wait(bar, 11 + jnp.where(crosses, 1, 0))

    lo, up = pl.ds(0, HALF), pl.ds(HALF, HALF)

    def own(j, rows, i):
        return remote(grad_in.at[rows], gath.at[t, rows], g_s.at[i], g_r.at[i], (s, row(j), d))

    def onward(start, j, rows, i):
        k = row(start)
        return remote(gath.at[k, rows], gath.at[k, rows], g_s.at[i], g_r.at[i], (s, row(j), d))

    p2 = [own(2, lo, 0), own(2, up, 1)]
    m2 = [own(-2, lo, 2), own(-2, up, 3)]
    p1, m1 = own(1, pl.ds(0, SEQ), 4), own(-1, pl.ds(0, SEQ), 5)
    p3 = [onward(-2, 1, lo, 6), onward(-2, 1, up, 7)]
    m3 = [onward(2, -1, lo, 8), onward(2, -1, up, 9)]
    p4, m4 = onward(-2, 2, lo, 10), onward(2, -2, up, 11)

    p2[0].start()
    m2[1].start()
    p2[1].start()
    m2[0].start()
    p1.start()
    m1.start()

    def beside(j, i):
        k = row(j)
        return remote(gath.at[k], gath.at[k], b_s.at[i], b_r.at[i], (s, sib, d))

    ring = (0, 1, -1, 2, -2, 3, -3, 4)
    besides = {j: beside(j, i) for i, j in enumerate(ring)}

    tt = 2 * (y % 2) + c

    def quarter(m):
        q = lax.rem(y // 2 + m, 4)
        k = row(2 * m)
        return q != d, remote(gath.at[k], gd.at[tt, d], z_s.at[m], z_r.at[d], (s, t, q))

    def send_quarter(m):
        away, copy = quarter(m)

        @pl.when(away)
        def _():
            copy.start()

    locals_[2].wait()
    besides[0].start()
    send_quarter(0)

    locals_[1].wait()
    below = (s - 1, t, d)
    early = remote(qkv_in, qkv_u, e_s.at[0], e_r.at[0], below)
    pos_copy = remote(pos_o, pos_u, e_s.at[1], e_r.at[1], below)
    cross = remote(qkv_in.at[pl.ds(0, 3)], qkv_u.at[pl.ds(0, 3)], e_s.at[0], e_r.at[0], below)

    def part(p):
        return pl.ds(1 + 2 * p, 2)

    def to_plane(p):
        return remote(qkv_in.at[part(p)], relay, e_s.at[1 + p], e_r.at[5], (base + p, t, d))

    def from_plane(p):
        return remote(relay, qkv_u.at[part(p)], e_s.at[5], e_r.at[1 + p], (base - 1, t, d))

    @pl.when(x > 0)
    def _():
        early.start()
        pos_copy.start()

    @pl.when(jnp.logical_and(x == 0, crosses))
    def _():
        for p in (1, 2, 3):
            to_plane(p).start()
        cross.start()
        remote(pos_o, pos_u, e_s.at[6], e_r.at[1], below).start()

    locals_[0].wait()
    for h in range(NH):
        p = probs_t(qkv_o, pos_o, h).astype(BF16)
        att[d, :, h * DH:(h + 1) * DH] = dot(p, qkv_o[2 * NH + h], 0, 0).astype(BF16)
    att_copies = [
        remote(att.at[d], att.at[d], a_s.at[i], a_r.at[d], (s, t, lax.rem(d + i, 4))) for i in (1, 2, 3)
    ]
    for copy in att_copies:
        copy.start()

    def add(k, first=False):
        rows = pl.ds(pl.multiple_of(k * COLS, COLS), COLS)
        value = jnp.dot(gath[k], w_v[rows, :], preferred_element_type=F32)
        acc[...] = value if first else acc[...] + value

    locals_[3].wait()
    add(row(0), first=True)

    p2[0].wait_recv()
    p4.start()
    p3[0].start()
    m2[1].wait_recv()
    m4.start()
    m3[1].start()
    p2[1].wait_recv()
    p3[1].start()
    besides[-2].start()
    m2[0].wait_recv()
    m3[0].start()
    besides[2].start()
    send_quarter(1)
    send_quarter(3)
    p1.wait_recv()
    besides[-1].start()
    m1.wait_recv()
    besides[1].start()

    for p in (1, 2, 3):
        @pl.when(jnp.logical_and(x == p, crosses))
        def _(p=p):
            to_plane(p).wait_recv()
            from_plane(p).start()

    for j in (-2, 2, -1, 1):
        add(row(j))

    def other(j):
        besides[j].wait_recv()
        add(row(j, 1 - c))

    for j in (0, -2, 2, -1, 1):
        other(j)

    for q in p3:
        q.wait_recv()
    besides[-3].start()
    add(row(-3))
    for q in m3:
        q.wait_recv()
    besides[3].start()
    add(row(3))
    p4.wait_recv()
    m4.wait_recv()
    besides[4].start()
    send_quarter(2)
    add(row(4))
    for j in (-3, 3, 4):
        other(j)

    d_own[...] = acc[...].astype(BF16)
    late = [remote(d_own.at[r], d_up.at[r], l_s.at[i], l_r.at[i], below) for i, r in enumerate((lo, up))]
    hop = remote(d_own.at[up], relay2, l_s.at[1], l_r.at[2], (base + 3, t, d))
    hop_on = remote(relay2, d_up.at[up], l_s.at[2], l_r.at[1], (base - 1, t, d))

    @pl.when(x > 0)
    def _():
        late[0].start()
        late[1].start()

    @pl.when(jnp.logical_and(x == 0, crosses))
    def _():
        hop.start()
        late[0].start()

    mine = [pltpu.make_async_copy(gath.at[4 * d + i], gd.at[i, d], loc.at[4 + i]) for i in range(4)]
    for copy in mine:
        copy.start()

    has_above = s < 15

    @pl.when(jnp.logical_and(has_above, x < 3))
    def _():
        early.wait_recv()

    @pl.when(jnp.logical_and(has_above, x == 3))
    def _():
        cross.wait_recv()
        for p in (1, 2, 3):
            from_plane(p).wait_recv()

    @pl.when(has_above)
    def _():
        pos_copy.wait_recv()
        for h in range(NH):
            p_up[h] = probs_t(qkv_u, pos_u, h)

    @pl.when(jnp.logical_and(x == 3, crosses))
    def _():
        hop.wait_recv()
        hop_on.start()

    pair = lax.rem(y + 1 - 2 * (y % 2), 8) * 2 + c
    tt2 = 2 * (1 - y % 2) + c
    there, side1, side2 = [], [], []
    for i in (1, 2, 3):
        r = lax.rem(d + i, 4)
        there.append(remote(gd.at[tt, r], gd.at[tt, r], x_s.at[i], x_r.at[r], (s, pair, d)))
        side1.append(remote(gd.at[tt, r], gd.at[tt, r], x_s.at[4 + i], x_r.at[4 + r], (s, sib, d)))
        side2.append(remote(gd.at[tt2, r], gd.at[tt2, r], x_s.at[8 + i], x_r.at[8 + r], (s, sib, d)))
    for i in (1, 2, 3):
        r = lax.rem(d + i, 4)
        remote(gath.at[0], gd.at[tt, r], z_s.at[0], z_r.at[r], (s, t, r)).wait_recv()
        there[i - 1].start()
        side1[i - 1].start()

    @pl.when(has_above)
    def _():
        for copy in late:
            copy.wait_recv()
        scale = 1.0 / math.sqrt(DH)
        for h in range(NH):
            p = p_up[h]
            da = d_up[:, h * DH:(h + 1) * DH]
            dp = dot(qkv_u[2 * NH + h], da, 1, 1)
            ds = (p * (dp - jnp.sum(p * dp, axis=0, keepdims=True))).astype(BF16)
            up_out[2 * NH + h] = dot(p.astype(BF16), da, 1, 0).astype(BF16)
            up_out[NH + h] = (dot(ds, qkv_u[h], 1, 0) * scale).astype(BF16)
            up_out[h] = (dot(ds, qkv_u[NH + h], 0, 0) * scale).astype(BF16)

    @pl.when(jnp.logical_not(has_above))
    def _():
        up_out[...] = jnp.zeros_like(up_out)

    for i in (1, 2, 3):
        r = lax.rem(d + i, 4)
        remote(gd.at[tt2, r], gd.at[tt2, r], x_s.at[i], x_r.at[r], (s, pair, d)).wait_recv()
        side2[i - 1].start()

    for copy in mine:
        copy.wait()
    for i in (1, 2, 3):
        r = lax.rem(d + i, 4)
        remote(att.at[r], att.at[r], a_s.at[i], a_r.at[r], (s, t, r)).wait_recv()
    for copy in side1 + side2:
        copy.wait_recv()
    rows = att[...].reshape(4 * SEQ, COLS)
    for i in range(4):
        dw_out[i * COLS:(i + 1) * COLS, :] = dot(gd[i].reshape(4 * SEQ, COLS), rows, 0, 0).astype(BF16)

    for copy in p2 + m2 + [p1, m1] + p3 + m3 + [p4, m4] + list(besides.values()) + att_copies:
        copy.wait_send()
    for copy in there + side1 + side2:
        copy.wait_send()
    for m in range(4):
        away, copy = quarter(m)

        @pl.when(away)
        def _(copy=copy):
            copy.wait_send()

    @pl.when(x > 0)
    def _():
        early.wait_send()
        pos_copy.wait_send()
        late[0].wait_send()
        late[1].wait_send()

    @pl.when(jnp.logical_and(x == 0, crosses))
    def _():
        for p in (1, 2, 3):
            to_plane(p).wait_send()
        cross.wait_send()
        remote(pos_o, pos_u, e_s.at[6], e_r.at[1], below).wait_send()
        hop.wait_send()
        late[0].wait_send()

    for p in (1, 2, 3):
        @pl.when(jnp.logical_and(x == p, crosses))
        def _(p=p):
            from_plane(p).wait_send()

    @pl.when(jnp.logical_and(x == 3, crosses))
    def _():
        hop_on.wait_send()


def local(saved_qkv, positions, w_out, grad_out):
    qkv = jnp.transpose(saved_qkv[0, 0], (0, 2, 1, 3)).reshape(3 * NH, SEQ, DH)
    sems = pltpu.SemaphoreType.DMA
    any_, vmem = pl.BlockSpec(memory_space=pl.ANY), pl.BlockSpec(memory_space=pltpu.VMEM)
    dw, up = pl.pallas_call(
        kernel,
        out_shape=(
            jax.ShapeDtypeStruct((4 * COLS, COLS), BF16),
            jax.ShapeDtypeStruct((3 * NH, SEQ, DH), BF16),
        ),
        in_specs=[any_] * 4,
        out_specs=(vmem, vmem),
        scratch_shapes=[
            pltpu.VMEM((16, SEQ, COLS), BF16),
            pltpu.VMEM((16 * COLS, COLS), BF16),
            pltpu.VMEM((3 * NH, SEQ, DH), BF16),
            pltpu.VMEM((1, SEQ), jnp.int32),
            pltpu.VMEM((3 * NH, SEQ, DH), BF16),
            pltpu.VMEM((1, SEQ), jnp.int32),
            pltpu.VMEM((2, SEQ, DH), BF16),
            pltpu.VMEM((HALF, COLS), BF16),
            pltpu.VMEM((4, SEQ, COLS), BF16),
            pltpu.VMEM((4, 4, SEQ, COLS), BF16),
            pltpu.VMEM((SEQ, COLS), F32),
            pltpu.VMEM((SEQ, COLS), BF16),
            pltpu.VMEM((SEQ, COLS), BF16),
            pltpu.VMEM((NH, SEQ, SEQ), F32),
            sems((8,)), sems((12,)), sems((12,)), sems((8,)), sems((8,)), sems((4,)), sems((4,)),
            sems((4,)), sems((4,)), sems((7,)), sems((6,)), sems((3,)), sems((3,)), sems((12,)), sems((12,)),
        ],
        compiler_params=pltpu.CompilerParams(
            collective_id=0, has_side_effects=True, vmem_limit_bytes=VMEM_LIMIT
        ),
        cost_estimate=pl.CostEstimate(flops=1_300_000_000, bytes_accessed=7_000_000, transcendentals=100_000),
    )(qkv, positions[0], w_out[0], grad_out[0, 0])
    up = jnp.transpose(up.reshape(3, NH, SEQ, DH), (0, 2, 1, 3))
    return dw[None], up[None, None]


def solution(mesh):
    in_specs = (
        P("section", "dp", None, None, "st", None),
        P("section", "dp", None),
        P("section", None, "st"),
        P("section", "dp", None, "st"),
    )
    out_specs = (P("section", "dp", "st"), P("section", "dp", None, None, "st", None))
    return jax.shard_map(local, mesh=mesh, in_specs=in_specs, out_specs=out_specs, check_vma=False)
```

time: 193 us -> 58.9 us (0.31)
  the two profiles are of different devices: /device:TPU:1 before, /device:TPU:143 now
where the time goes in v1:
time: 58.9 us; the launch traced here: 58.8 us
  Pallas kernels  54.9 us (93%)
  local copies, waits for them, and re-layouts  3.16 us (5%)
  between operations  0.65 us (1%)
    pallas_call x1, Pallas kernels, local(): pl.pallas_call(kernel, out_shape=(jax.ShapeDtypeStruct((4 * COLS, COLS),...  54.9 us
    unnamed x4, local copies, waits for them, and re-layouts  3.16 us

profile of v1, /device:TPU:143, one launch (start us, length us, event | category | flops | bytes accessed | tf_op | source)
XLA Modules:
  0.0 58.8 jit_solution(13627785875475441470)
XLA Ops:
  0.6 54.9 %shard_map.59 = (bf16[1536,384]{1,0:T(8,128)(2,1)}, bf16[9,128,128]{2,1,0:T(8,128)(2,1)}) custom-call(bf16[9,128,128]{2,1,0:T(8,128)(2,1)} %bitcast.17, s32[1,128]{1,0:T(1,128)} %bitcast.19, bf16[6144,384]{1,0:T(8,128)(2,1)} %bitcast.14, bf16[128,384]{1,0:T(8,128)(2,1)} %bitcast.18), custom_call_target="tpu_custom_call" | custom-call | flops 1300000000 | bytes 7000000 | tf_op jit(solution)/shard_map/pallas_call | solution.py:352
  55.6 0.0 copy-start
  55.6 2.4 %copy.8 = bf16[1,1536,384]{2,1,0:T(8,128)(2,1)} copy(bf16[1,1536,384]{2,1,0:T(8,128)(2,1)} %bitcast.15) | data formatting | bytes 2359296
  58.0 0.0 copy-done
  58.0 0.7 %copy.9 = bf16[1,1,3,128,3,128]{5,3,4,2,1,0:T(8,128)(2,1)} copy(bf16[1,1,3,128,3,128]{5,3,4,2,1,0:T(8,128)(2,1)S(1)} %bitcast.16) | data formatting | bytes 589824
Async XLA Ops:
  55.6 2.5 %copy-start = (bf16[9,128,128]{2,1,0:T(8,128)(2,1)S(1)}, bf16[9,128,128]{2,1,0:T(8,128)(2,1)}, u32[]{:S(2)}) copy-start(bf16[9,128,128]{2,1,0:T(8,128)(2,1)} %get-tuple-element.5) | copy-start | bytes 884740

commit v2 on v1

--- a/solution.py
+++ b/solution.py
@@ -11,7 +11,7 @@
 F32, BF16 = jnp.float32, jnp.bfloat16
 SEQ, DH, NH, COLS = 128, 128, 3, 384
 HALF = SEQ // 2
-VMEM_LIMIT = 56 * 2**20
+VMEM_LIMIT = 32 * 2**20
 
 
 def dot(a, b, ca, cb):
@@ -56,7 +56,14 @@
     greet((s, sib, d))
     for i in (1, 2, 3):
         greet((s, t, lax.rem(d + i, 4)))
-        greet((base + lax.rem(x + i, 4), t, d))
+
+    @pl.when(x < 3)
+    def _():
+        greet((s + 1, t, d))
+
+    @pl.when(jnp.logical_and(x > 0, crosses))
+    def _():
+        greet((base, t, d))
 
     @pl.when(jnp.logical_and(x == 3, hi < 3))
     def _():
@@ -72,7 +79,7 @@
     for copy in locals_:
         copy.start()
 
-    pl.semaphore_wait(bar, 11 + jnp.where(crosses, 1, 0))
+    pl.semaphore_wait(bar, 8 + jnp.where(x > 0, 1, 0) + jnp.where(crosses, jnp.where(x > 0, 1, 4), 0))
 
     lo, up = pl.ds(0, HALF), pl.ds(HALF, HALF)
 
@@ -153,11 +160,31 @@
     for h in range(NH):
         p = probs_t(qkv_o, pos_o, h).astype(BF16)
         att[d, :, h * DH:(h + 1) * DH] = dot(p, qkv_o[2 * NH + h], 0, 0).astype(BF16)
-    att_copies = [
-        remote(att.at[d], att.at[d], a_s.at[i], a_r.at[d], (s, t, lax.rem(d + i, 4))) for i in (1, 2, 3)
-    ]
-    for copy in att_copies:
-        copy.start()
+
+    def pass_att(k, step, i):
+        r = d - k * step
+        return remote(att.at[r], att.at[r], a_s.at[i], a_r.at[r], (s, t, d + step))
+
+    lines = ((1, d < 3), (-1, d > 0))
+
+    def source(k, step):
+        return (d >= k) if step == 1 else (d + k < 4)
+
+    for i, (step, more) in enumerate(lines):
+        @pl.when(more)
+        def _(i=i, step=step):
+            pass_att(0, step, i).start()
+
+    def relay_att(k):
+        for i, (step, more) in enumerate(lines):
+            @pl.when(source(k, step))
+            def _(step=step):
+                pass_att(k, step, 0).wait_recv()
+
+            if k < 3:
+                @pl.when(jnp.logical_and(source(k, step), more))
+                def _(i=i, step=step):
+                    pass_att(k, step, 2 * k + i).start()
 
     def add(k, first=False):
         rows = pl.ds(pl.multiple_of(k * COLS, COLS), COLS)
@@ -201,6 +228,7 @@
 
     for j in (0, -2, 2, -1, 1):
         other(j)
+    relay_att(1)
 
     for q in p3:
         q.wait_recv()
@@ -220,7 +248,7 @@
 
     d_own[...] = acc[...].astype(BF16)
     late = [remote(d_own.at[r], d_up.at[r], l_s.at[i], l_r.at[i], below) for i, r in enumerate((lo, up))]
-    hop = remote(d_own.at[up], relay2, l_s.at[1], l_r.at[2], (base + 3, t, d))
+    hop = remote(d_own.at[up], relay2, l_s.at[1], l_r.at[2], (base + 1, t, d))
     hop_on = remote(relay2, d_up.at[up], l_s.at[2], l_r.at[1], (base - 1, t, d))
 
     @pl.when(x > 0)
@@ -239,43 +267,12 @@
 
     has_above = s < 15
 
-    @pl.when(jnp.logical_and(has_above, x < 3))
-    def _():
-        early.wait_recv()
-
-    @pl.when(jnp.logical_and(has_above, x == 3))
-    def _():
-        cross.wait_recv()
-        for p in (1, 2, 3):
-            from_plane(p).wait_recv()
-
-    @pl.when(has_above)
-    def _():
+    def softmax_above():
         pos_copy.wait_recv()
         for h in range(NH):
             p_up[h] = probs_t(qkv_u, pos_u, h)
 
-    @pl.when(jnp.logical_and(x == 3, crosses))
-    def _():
-        hop.wait_recv()
-        hop_on.start()
-
-    pair = lax.rem(y + 1 - 2 * (y % 2), 8) * 2 + c
-    tt2 = 2 * (1 - y % 2) + c
-    there, side1, side2 = [], [], []
-    for i in (1, 2, 3):
-        r = lax.rem(d + i, 4)
-        there.append(remote(gd.at[tt, r], gd.at[tt, r], x_s.at[i], x_r.at[r], (s, pair, d)))
-        side1.append(remote(gd.at[tt, r], gd.at[tt, r], x_s.at[4 + i], x_r.at[4 + r], (s, sib, d)))
-        side2.append(remote(gd.at[tt2, r], gd.at[tt2, r], x_s.at[8 + i], x_r.at[8 + r], (s, sib, d)))
-    for i in (1, 2, 3):
-        r = lax.rem(d + i, 4)
-        remote(gath.at[0], gd.at[tt, r], z_s.at[0], z_r.at[r], (s, t, r)).wait_recv()
-        there[i - 1].start()
-        side1[i - 1].start()
-
-    @pl.when(has_above)
-    def _():
+    def backward_above():
         for copy in late:
             copy.wait_recv()
         scale = 1.0 / math.sqrt(DH)
@@ -288,27 +285,61 @@
             up_out[NH + h] = (dot(ds, qkv_u[h], 1, 0) * scale).astype(BF16)
             up_out[h] = (dot(ds, qkv_u[NH + h], 0, 0) * scale).astype(BF16)
 
-    @pl.when(jnp.logical_not(has_above))
-    def _():
-        up_out[...] = jnp.zeros_like(up_out)
-
-    for i in (1, 2, 3):
-        r = lax.rem(d + i, 4)
+    @pl.when(x < 3)
+    def _():
+        early.wait_recv()
+        softmax_above()
+
+    @pl.when(jnp.logical_and(x == 1, crosses))
+    def _():
+        hop.wait_recv()
+        hop_on.start()
+
+    relay_att(2)
+
+    pair = (y + 1 - 2 * (y % 2)) * 2 + c
+    tt2 = 2 * (1 - y % 2) + c
+    others = (d + 1 - 2 * (d % 2), 2 - d // 2, 3 - 3 * (d // 2))
+    there, side1, side2 = [], [], []
+    for i, r in enumerate(others):
+        there.append(remote(gd.at[tt, r], gd.at[tt, r], x_s.at[i], x_r.at[r], (s, pair, d)))
+        side1.append(remote(gd.at[tt, r], gd.at[tt, r], x_s.at[4 + i], x_r.at[4 + r], (s, sib, d)))
+        side2.append(remote(gd.at[tt2, r], gd.at[tt2, r], x_s.at[8 + i], x_r.at[8 + r], (s, sib, d)))
+    for i, r in enumerate(others):
+        remote(gath.at[0], gd.at[tt, r], z_s.at[0], z_r.at[r], (s, t, r)).wait_recv()
+        there[i].start()
+        side1[i].start()
+
+    @pl.when(x < 3)
+    def _():
+        backward_above()
+
+    for i, r in enumerate(others):
         remote(gd.at[tt2, r], gd.at[tt2, r], x_s.at[i], x_r.at[r], (s, pair, d)).wait_recv()
-        side2[i - 1].start()
+        side2[i].start()
 
     for copy in mine:
         copy.wait()
-    for i in (1, 2, 3):
-        r = lax.rem(d + i, 4)
-        remote(att.at[r], att.at[r], a_s.at[i], a_r.at[r], (s, t, r)).wait_recv()
+    relay_att(3)
     for copy in side1 + side2:
         copy.wait_recv()
     rows = att[...].reshape(4 * SEQ, COLS)
     for i in range(4):
         dw_out[i * COLS:(i + 1) * COLS, :] = dot(gd[i].reshape(4 * SEQ, COLS), rows, 0, 0).astype(BF16)
 
-    for copy in p2 + m2 + [p1, m1] + p3 + m3 + [p4, m4] + list(besides.values()) + att_copies:
+    @pl.when(jnp.logical_and(x == 3, has_above))
+    def _():
+        cross.wait_recv()
+        for p in (1, 2, 3):
+            from_plane(p).wait_recv()
+        softmax_above()
+        backward_above()
+
+    @pl.when(jnp.logical_not(has_above))
+    def _():
+        up_out[...] = jnp.zeros_like(up_out)
+
+    for copy in p2 + m2 + [p1, m1] + p3 + m3 + [p4, m4] + list(besides.values()):
         copy.wait_send()
     for copy in there + side1 + side2:
         copy.wait_send()
@@ -318,6 +349,12 @@
         @pl.when(away)
         def _(copy=copy):
             copy.wait_send()
+
+    for k in range(3):
+        for i, (step, more) in enumerate(lines):
+            @pl.when(jnp.logical_and(source(k, step), more))
+            def _(k=k, i=i, step=step):
+                pass_att(k, step, 2 * k + i).wait_send()
 
     @pl.when(x > 0)
     def _():
@@ -340,7 +377,7 @@
         def _(p=p):
             from_plane(p).wait_send()
 
-    @pl.when(jnp.logical_and(x == 3, crosses))
+    @pl.when(jnp.logical_and(x == 1, crosses))
     def _():
         hop_on.wait_send()
 
@@ -373,13 +410,13 @@
             pltpu.VMEM((SEQ, COLS), BF16),
             pltpu.VMEM((NH, SEQ, SEQ), F32),
             sems((8,)), sems((12,)), sems((12,)), sems((8,)), sems((8,)), sems((4,)), sems((4,)),
-            sems((4,)), sems((4,)), sems((7,)), sems((6,)), sems((3,)), sems((3,)), sems((12,)), sems((12,)),
+            sems((6,)), sems((4,)), sems((7,)), sems((6,)), sems((3,)), sems((3,)), sems((12,)), sems((12,)),
         ],
         compiler_params=pltpu.CompilerParams(
             collective_id=0, has_side_effects=True, vmem_limit_bytes=VMEM_LIMIT
         ),
         cost_estimate=pl.CostEstimate(flops=1_300_000_000, bytes_accessed=7_000_000, transcendentals=100_000),
-    )(qkv, positions[0], w_out[0], grad_out[0, 0])
+    )(*(pltpu.with_memory_space_constraint(a, pltpu.HBM) for a in (qkv, positions[0], w_out[0], grad_out[0, 0])))
     up = jnp.transpose(up.reshape(3, NH, SEQ, DH), (0, 2, 1, 3))
     return dw[None], up[None, None]
 

time: 58.9 us -> 48.2 us (0.82)
  the two profiles are of different devices: /device:TPU:143 before, /device:TPU:291 now
where the time goes in v2:
time: 48.2 us; the launch traced here: 48 us
  Pallas kernels  45.6 us (95%)
  local copies, waits for them, and re-layouts  1.73 us (4%)
  between operations  0.64 us (1%)
    pallas_call x1, Pallas kernels, local(): pl.pallas_call(kernel, out_shape=(jax.ShapeDtypeStruct((4 * COLS, COLS),...  45.6 us
    unnamed x2, local copies, waits for them, and re-layouts  1.73 us

profile of v2, /device:TPU:291, one launch (start us, length us, event | category | flops | bytes accessed | tf_op | source)
XLA Modules:
  0.0 48.0 jit_solution(13172075700738522429)
XLA Ops:
  0.6 45.6 %shard_map.59 = (bf16[1536,384]{1,0:T(8,128)(2,1)S(1)}, bf16[9,128,128]{2,1,0:T(8,128)(2,1)S(1)}) custom-call(bf16[9,128,128]{2,1,0:T(8,128)(2,1)} %bitcast.17, s32[1,128]{1,0:T(1,128)} %bitcast.19, bf16[6144,384]{1,0:T(8,128)(2,1)} %bitcast.16, bf16[128,384]{1,0:T(8,128)(2,1)} %bitcast.18), custom_call_target="tpu_custom_call" | custom-call | flops 1300000000 | bytes 7000000 | tf_op jit(solution)/shard_map/pallas_call | solution.py:389
  46.3 1.0 %copy.8 = bf16[1,1536,384]{2,1,0:T(8,128)(2,1)} copy(bf16[1,1536,384]{2,1,0:T(8,128)(2,1)S(1)} %bitcast.14) | data formatting | bytes 2359296
  47.3 0.7 %copy.9 = bf16[1,1,3,128,3,128]{5,3,4,2,1,0:T(8,128)(2,1)} copy(bf16[1,1,3,128,3,128]{5,3,4,2,1,0:T(8,128)(2,1)S(1)} %bitcast.15) | data formatting | bytes 589824

commit v3 on v2

--- a/solution.py
+++ b/solution.py
@@ -11,6 +11,7 @@
 F32, BF16 = jnp.float32, jnp.bfloat16
 SEQ, DH, NH, COLS = 128, 128, 3, 384
 HALF = SEQ // 2
+NEAR = 80
 VMEM_LIMIT = 32 * 2**20
 
 
@@ -247,9 +248,10 @@
         other(j)
 
     d_own[...] = acc[...].astype(BF16)
-    late = [remote(d_own.at[r], d_up.at[r], l_s.at[i], l_r.at[i], below) for i, r in enumerate((lo, up))]
-    hop = remote(d_own.at[up], relay2, l_s.at[1], l_r.at[2], (base + 1, t, d))
-    hop_on = remote(relay2, d_up.at[up], l_s.at[2], l_r.at[1], (base - 1, t, d))
+    near, far = pl.ds(0, NEAR), pl.ds(NEAR, SEQ - NEAR)
+    late = [remote(d_own.at[r], d_up.at[r], l_s.at[i], l_r.at[i], below) for i, r in enumerate((near, far))]
+    hop = remote(d_own.at[far], relay2, l_s.at[1], l_r.at[2], (base + 3, t, d))
+    hop_on = remote(relay2, d_up.at[far], l_s.at[2], l_r.at[1], (base - 1, t, d))
 
     @pl.when(x > 0)
     def _():
@@ -290,24 +292,38 @@
         early.wait_recv()
         softmax_above()
 
-    @pl.when(jnp.logical_and(x == 1, crosses))
+    @pl.when(jnp.logical_and(x == 3, crosses))
     def _():
         hop.wait_recv()
         hop_on.start()
 
     relay_att(2)
 
-    pair = (y + 1 - 2 * (y % 2)) * 2 + c
+    turn = 1 - 2 * (y % 2)
+    pair, outer = row(turn), row(-turn)
     tt2 = 2 * (1 - y % 2) + c
     others = (d + 1 - 2 * (d % 2), 2 - d // 2, 3 - 3 * (d // 2))
-    there, side1, side2 = [], [], []
-    for i, r in enumerate(others):
-        there.append(remote(gd.at[tt, r], gd.at[tt, r], x_s.at[i], x_r.at[r], (s, pair, d)))
-        side1.append(remote(gd.at[tt, r], gd.at[tt, r], x_s.at[4 + i], x_r.at[4 + r], (s, sib, d)))
-        side2.append(remote(gd.at[tt2, r], gd.at[tt2, r], x_s.at[8 + i], x_r.at[8 + r], (s, sib, d)))
+    whole = pl.ds(0, SEQ)
+
+    def swap(tile):
+        cuts = ((0, whole, pair), (1, whole, outer), (2, lo, pair), (2, up, outer))
+        return [
+            remote(gd.at[tile, others[i], rows], gd.at[tile, others[i], rows], x_s.at[n], x_r.at[n], (s, dev, d))
+            for n, (i, rows, dev) in enumerate(cuts)
+        ]
+
+    def across(tile, n):
+        return [
+            remote(gd.at[tile, r], gd.at[tile, r], x_s.at[n + i], x_r.at[n + i], (s, sib, d))
+            for i, r in enumerate(others)
+        ]
+
+    there, missing, side1, side2 = swap(tt), swap(tt2), across(tt, 4), across(tt2, 8)
+    sent_on = ((0,), (1,), (2, 3))
     for i, r in enumerate(others):
         remote(gath.at[0], gd.at[tt, r], z_s.at[0], z_r.at[r], (s, t, r)).wait_recv()
-        there[i].start()
+        for n in sent_on[i]:
+            there[n].start()
         side1[i].start()
 
     @pl.when(x < 3)
@@ -315,7 +331,8 @@
         backward_above()
 
     for i, r in enumerate(others):
-        remote(gd.at[tt2, r], gd.at[tt2, r], x_s.at[i], x_r.at[r], (s, pair, d)).wait_recv()
+        for n in sent_on[i]:
+            missing[n].wait_recv()
         side2[i].start()
 
     for copy in mine:
@@ -377,7 +394,7 @@
         def _(p=p):
             from_plane(p).wait_send()
 
-    @pl.when(jnp.logical_and(x == 1, crosses))
+    @pl.when(jnp.logical_and(x == 3, crosses))
     def _():
         hop_on.wait_send()
 
@@ -402,7 +419,7 @@
             pltpu.VMEM((3 * NH, SEQ, DH), BF16),
             pltpu.VMEM((1, SEQ), jnp.int32),
             pltpu.VMEM((2, SEQ, DH), BF16),
-            pltpu.VMEM((HALF, COLS), BF16),
+            pltpu.VMEM((SEQ - NEAR, COLS), BF16),
             pltpu.VMEM((4, SEQ, COLS), BF16),
             pltpu.VMEM((4, 4, SEQ, COLS), BF16),
             pltpu.VMEM((SEQ, COLS), F32),

time: 48.2 us -> 46.7 us (0.969)
  the two profiles are of different devices: /device:TPU:291 before, /device:TPU:281 now
where the time goes in v3:
time: 46.7 us; the launch traced here: 46.5 us
  Pallas kernels  44.2 us (95%)
  local copies, waits for them, and re-layouts  1.73 us (4%)
  between operations  0.64 us (1%)
    pallas_call x1, Pallas kernels, local(): pl.pallas_call(kernel, out_shape=(jax.ShapeDtypeStruct((4 * COLS, COLS),...  44.2 us
    unnamed x2, local copies, waits for them, and re-layouts  1.73 us

profile of v3, /device:TPU:281, one launch (start us, length us, event | category | flops | bytes accessed | tf_op | source)
XLA Modules:
  0.0 46.5 jit_solution(9728167398351902573)
XLA Ops:
  0.6 44.2 %shard_map.59 = (bf16[1536,384]{1,0:T(8,128)(2,1)S(1)}, bf16[9,128,128]{2,1,0:T(8,128)(2,1)S(1)}) custom-call(bf16[9,128,128]{2,1,0:T(8,128)(2,1)} %bitcast.17, s32[1,128]{1,0:T(1,128)} %bitcast.19, bf16[6144,384]{1,0:T(8,128)(2,1)} %bitcast.16, bf16[128,384]{1,0:T(8,128)(2,1)} %bitcast.18), custom_call_target="tpu_custom_call" | custom-call | flops 1300000000 | bytes 7000000 | tf_op jit(solution)/shard_map/pallas_call | solution.py:406
  44.8 1.0 %copy.8 = bf16[1,1536,384]{2,1,0:T(8,128)(2,1)} copy(bf16[1,1536,384]{2,1,0:T(8,128)(2,1)S(1)} %bitcast.14) | data formatting | bytes 2359296
  45.8 0.7 %copy.9 = bf16[1,1,3,128,3,128]{5,3,4,2,1,0:T(8,128)(2,1)} copy(bf16[1,1,3,128,3,128]{5,3,4,2,1,0:T(8,128)(2,1)S(1)} %bitcast.15) | data formatting | bytes 589824

commit v4 on v3

--- a/solution.py
+++ b/solution.py
@@ -12,6 +12,7 @@
 SEQ, DH, NH, COLS = 128, 128, 3, 384
 HALF = SEQ // 2
 NEAR = 80
+PLANES = {1: (1, 3), 2: (4, 3), 3: (7, 2)}
 VMEM_LIMIT = 32 * 2**20
 
 
@@ -134,16 +135,16 @@
     below = (s - 1, t, d)
     early = remote(qkv_in, qkv_u, e_s.at[0], e_r.at[0], below)
     pos_copy = remote(pos_o, pos_u, e_s.at[1], e_r.at[1], below)
-    cross = remote(qkv_in.at[pl.ds(0, 3)], qkv_u.at[pl.ds(0, 3)], e_s.at[0], e_r.at[0], below)
+    cross = remote(qkv_in.at[pl.ds(0, 1)], qkv_u.at[pl.ds(0, 1)], e_s.at[0], e_r.at[0], below)
 
     def part(p):
-        return pl.ds(1 + 2 * p, 2)
+        return pl.ds(*PLANES[p])
 
     def to_plane(p):
-        return remote(qkv_in.at[part(p)], relay, e_s.at[1 + p], e_r.at[5], (base + p, t, d))
+        return remote(qkv_in.at[part(p)], relay.at[pl.ds(0, PLANES[p][1])], e_s.at[1 + p], e_r.at[5], (base + p, t, d))
 
     def from_plane(p):
-        return remote(relay, qkv_u.at[part(p)], e_s.at[5], e_r.at[1 + p], (base - 1, t, d))
+        return remote(relay.at[pl.ds(0, PLANES[p][1])], qkv_u.at[part(p)], e_s.at[5], e_r.at[1 + p], (base - 1, t, d))
 
     @pl.when(x > 0)
     def _():
@@ -418,7 +419,7 @@
             pltpu.VMEM((1, SEQ), jnp.int32),
             pltpu.VMEM((3 * NH, SEQ, DH), BF16),
             pltpu.VMEM((1, SEQ), jnp.int32),
-            pltpu.VMEM((2, SEQ, DH), BF16),
+            pltpu.VMEM((3, SEQ, DH), BF16),
             pltpu.VMEM((SEQ - NEAR, COLS), BF16),
             pltpu.VMEM((4, SEQ, COLS), BF16),
             pltpu.VMEM((4, 4, SEQ, COLS), BF16),

time: 46.7 us -> 45.9 us (0.983)
  the two profiles are of different devices: /device:TPU:281 before, /device:TPU:311 now
where the time goes in v4:
time: 45.9 us; the launch traced here: 45.7 us
  Pallas kernels  43.4 us (95%)
  local copies, waits for them, and re-layouts  1.73 us (4%)
  between operations  0.64 us (1%)
    pallas_call x1, Pallas kernels, local(): pl.pallas_call(kernel, out_shape=(jax.ShapeDtypeStruct((4 * COLS, COLS),...  43.4 us
    unnamed x2, local copies, waits for them, and re-layouts  1.73 us

profile of v4, /device:TPU:311, one launch (start us, length us, event | category | flops | bytes accessed | tf_op | source)
XLA Modules:
  0.0 45.7 jit_solution(13129998541017005661)
XLA Ops:
  0.6 43.4 %shard_map.59 = (bf16[1536,384]{1,0:T(8,128)(2,1)S(1)}, bf16[9,128,128]{2,1,0:T(8,128)(2,1)S(1)}) custom-call(bf16[9,128,128]{2,1,0:T(8,128)(2,1)} %bitcast.17, s32[1,128]{1,0:T(1,128)} %bitcast.19, bf16[6144,384]{1,0:T(8,128)(2,1)} %bitcast.16, bf16[128,384]{1,0:T(8,128)(2,1)} %bitcast.18), custom_call_target="tpu_custom_call" | custom-call | flops 1300000000 | bytes 7000000 | tf_op jit(solution)/shard_map/pallas_call | solution.py:407
  44.0 1.0 %copy.8 = bf16[1,1536,384]{2,1,0:T(8,128)(2,1)} copy(bf16[1,1536,384]{2,1,0:T(8,128)(2,1)S(1)} %bitcast.14) | data formatting | bytes 2359296
  45.0 0.7 %copy.9 = bf16[1,1,3,128,3,128]{5,3,4,2,1,0:T(8,128)(2,1)} copy(bf16[1,1,3,128,3,128]{5,3,4,2,1,0:T(8,128)(2,1)S(1)} %bitcast.15) | data formatting | bytes 589824
